TPU v7x, 256 devices: a whole 4x4x8 slice. The times are simulated.
256 devices in a mesh: seq: 16 (over y, z_lo, core), chan: 16 (over z_hi, x).
Axes of the slice: x: 4, y: 4, z: 8 (z_hi: 4, z_lo: 2; z = z_hi * 2 + z_lo), core: 2. Of those that a mesh axis runs over, the one named last changes fastest.
Arguments:
- key_proj: bfloat16 [8192, 4096], P('seq', 'chan'), may hold values from -6 to 6
- value_proj: bfloat16 [8192, 4096], P('seq', 'chan'), may hold values from -6 to 6
- grad_out: bfloat16 [8192, 4096], P('seq', 'chan'), may hold values from -6 to 6
- filter_taps: bfloat16 [8192, 256], P('seq'), may hold values from -0.0625 to 0.0625
- skip_gain: float32 [4096], P('chan'), may hold values from -4 to 4
Outputs:
- key_grad: bfloat16 [8192, 4096], P('seq', 'chan')
- value_grad: bfloat16 [8192, 4096], P('seq', 'chan')
- filter_grad: float32 [8192, 256], P(('seq', 'chan'))
- bias_grad: float32 [4096], P(('chan', 'seq'))
All inputs are finite; a program needn't handle non-finite values.
Results may differ from a plain program's by a relative error of at most 0.009.
Values may be sent and summed in bfloat16 or wider, within the bound.
A program may use at most 128 MiB of HBM per device.

v0:
```python
import functools
import math

import jax
import jax.numpy as jnp
from jax import lax
from jax.experimental import pallas as pl
from jax.experimental.pallas import tpu as pltpu
from jax.sharding import PartitionSpec as P

MESH = pl.DeviceIdType.MESH
F32, BF16 = jnp.float32, jnp.bfloat16
NT = (((1,), (1,)), ((), ()))


def dot_nt(a, b):
    return lax.dot_general(a, b, NT, preferred_element_type=F32)


def iotas(rows, cols=128):
    lane = lax.broadcasted_iota(jnp.int32, (rows, cols), 1)
    return lane, lax.broadcasted_iota(jnp.int32, (rows, cols), 0)


def eye(size):
    lane, row = iotas(size, size)
    return jnp.where(lane == row, 1.0, 0.0).astype(BF16)


def halves(low, high):
    sub = lax.broadcasted_iota(jnp.int32, low.shape, 1)
    return jnp.where(sub < 4, low, high)


def turn(rows):
    return pltpu.roll(rows, 4, 1)


def to_tiles(block, tiles):
    flipped = dot_nt(eye(256), block).reshape(32, 8, 512)
    v = [flipped[:, :, 128 * jj : 128 * jj + 128] for jj in range(4)]
    even = jnp.concatenate([halves(v[0], turn(v[1])), halves(v[2], turn(v[3]))], axis=1)
    odd = jnp.concatenate([halves(turn(v[0]), v[1]), halves(turn(v[2]), v[3])], axis=1)
    tiles[...] = jnp.stack([even, odd], axis=1).reshape(64, 16, 128).astype(BF16)


def from_tiles(tiles):
    pairs = tiles[...].astype(F32).reshape(32, 32, 128)
    e0, e1, o0, o1 = (pairs[:, 8 * i : 8 * i + 8, :] for i in range(4))
    v = [halves(e0, turn(o0)), halves(turn(e0), o0), halves(e1, turn(o1)), halves(turn(e1), o1)]
    return [dot_nt(eye(128), one.reshape(256, 128).astype(BF16)) for one in v]


def unpack_tiles(src, dst, base, count):
    def one(i, c):
        rows = pl.ds(pl.multiple_of(base + 128 * i, 8), 128)
        dst[rows, :] = src[pl.ds(8 * i, 8)].astype(F32).reshape(128, 128)
        return c

    lax.fori_loop(0, count // 8, one, 0)


def build_toeplitz(h32, f, t_ref):
    lane, row = iotas(128)
    mask = lane + row < 128

    def one(e, c):
        rows = [h32[pl.ds(8 + 4 * (8 * e + i - 1) + f, 1), :] for i in range(9)]
        for i in range(8):
            before = jnp.broadcast_to(rows[i], (128, 128))
            here = jnp.broadcast_to(rows[i + 1], (128, 128))
            t = pltpu.roll(jnp.where(mask, here, before), 0, 1, stride=1, stride_axis=0)
            par, d0 = i // 4, i % 4
            t_ref[e, 128 * par : 128 * par + 128, 128 * d0 : 128 * d0 + 128] = t.astype(BF16)
        return c

    lax.fori_loop(0, 8, one, 0)


def build_gcat(g32, f, gcat, gt5):
    jj = lax.broadcasted_iota(jnp.int32, (256, 128), 0) % 4
    unit = eye(128)
    for d0 in range(5):
        block = g32[pl.ds(f + 4 * (d0 if d0 < 4 else 16), 256, stride=4), :]
        if 0 < d0 < 4:
            later = g32[pl.ds(f + 4 * (d0 + 12), 256, stride=4), :]
            block = jnp.where(jj + d0 < 4, block, later)
        block = block.astype(BF16)
        if d0 < 4:
            gcat[:, 128 * d0 : 128 * d0 + 128] = block
        gt5[128 * d0 : 128 * d0 + 128, :] = dot_nt(unit, block).astype(BF16)


def convolve(gcat, t_ref, acc):
    acc[...] = jnp.zeros_like(acc)
    for e in range(8):
        n = 256 - 32 * e
        y = dot_nt(gcat[32 * e : 256, :], t_ref[e])
        acc[0:n, :] += y[:, 0:128]
        acc[0 : n - 16, :] += y[16:, 128:256]


def build_rt(m32, f, mpad, rt):
    mpad[128:384, :] = m32[pl.ds(f, 256, stride=4), :].astype(BF16)
    lane, row = iotas(128)
    flip = jnp.where(lane == (row // 16) * 16 + 15 - row % 16, 1.0, 0.0).astype(BF16)
    for d in range(8):
        t = dot_nt(flip, mpad[128 - 16 * d : 384 - 16 * d, :]).astype(BF16)
        for a in range(8):
            piece = t[16 * a : 16 * a + 16, :]
            rt[16 * d : 16 * d + 16, 256 * a : 256 * a + 256] = piece
            rt[128 + 16 * d : 144 + 16 * d, 256 * a + 128 : 256 * a + 256] = piece[:, 0:128]


def correlate(rt, gt5, out):
    for half in range(2):
        acc = None
        for a in range(8):
            rows = gt5[16 * a + 256 * half : 16 * a + 256 * half + 256, :]
            y = dot_nt(rt[:, 256 * a : 256 * a + 256], rows)
            acc = y if acc is None else acc + y
        out[:, 256 * half : 256 * half + 256] = acc


def sum_diagonals(out, f, c_ref):
    lane, row = iotas(16)
    mask = lane + row >= 15
    after = jnp.zeros((16, 128), F32)
    for d1 in reversed(range(16)):
        for d0 in reversed(range(4)):
            here = out[16 * d1 : 16 * d1 + 16, 128 * d0 : 128 * d0 + 128]
            z = pltpu.roll(jnp.where(mask, here, after), 113, 1, stride=1, stride_axis=0)
            after = here
            c_ref[d0, pl.ds(4 * d1 + f, 1), :] = jnp.sum(z[0:8] + z[8:16], axis=0, keepdims=True)


def kernel(
    scales,
    key_ref,
    value_ref,
    grad_ref,
    taps_ref,
    gain_ref,
    key_out,
    value_out,
    filter_out,
    bias_out,
    g_send,
    m_send,
    h_send,
    b_send,
    g_recv,
    m_recv,
    h_recv,
    b_recv,
    y_send,
    y_recv,
    c_ref,
    c_recv,
    c_sum,
    c_last,
    g32,
    m32,
    h32,
    gcat,
    gt5,
    t_ref,
    acc,
    o32,
    mpad,
    rt,
    out,
    turned,
    sends,
    recvs,
):
    bias_scale, filter_scale = scales
    s, k = lax.axis_index("seq"), lax.axis_index("chan")
    y, c = s // 4, s % 4
    z, x = k // 4, k % 4
    me = 4 * s + x

    def group(i):
        s2 = (y + i // 16) % 4 * 4 + (c + i // 4 % 4) % 4
        x2 = (x + i % 4) % 4
        return (s2, 4 * z + x2), 4 * s2 + x2

    def row(i):
        s2 = (y + i // 4) % 4 * 4 + (c + i % 4) % 4
        return (s2, k), s2

    def column(i):
        z2 = (z + i) % 4
        return (s, 4 * z2 + x), z2

    def copy(src, dst, sem, device):
        return pltpu.make_async_remote_copy(
            src_ref=src,
            dst_ref=dst,
            send_sem=sends.at[sem],
            recv_sem=recvs.at[sem],
            device_id=device,
            device_id_type=MESH,
        )

    def all_of(src, dst, sem, count):
        return copy(src.at[pl.ds(0, count)], dst.at[pl.ds(0, count)], sem, group(1)[0])

    def each(lo, hi, body):
        lax.fori_loop(lo, hi, lambda i, none: (body(i), none)[1], 0)

    barrier = pltpu.get_barrier_semaphore()

    def greet(device):
        pl.semaphore_signal(barrier, inc=1, device_id=device, device_id_type=MESH)

    each(1, 64, lambda i: greet(group(i)[0]))
    each(1, 4, lambda i: greet(column(i)[0]))

    to_tiles(taps_ref[...], h_send)
    to_tiles(grad_ref[...], g_send)
    mixed = (key_ref[...].astype(F32) * value_ref[...].astype(F32)).astype(BF16)
    to_tiles(mixed, m_send)
    bias_part = jnp.sum(grad_ref[...].astype(F32) * mixed.astype(F32), axis=0, keepdims=True)
    b_send[...] = jnp.broadcast_to(bias_part, (8, 256))

    pl.semaphore_wait(barrier, 66)

    def send_taps(i):
        device, s2 = row(i)
        copy(h_send.at[4 * s2 + x], h_recv.at[s], 0, device).start()

    def send_grad(i):
        device, other = group(i)
        copy(g_send.at[other], g_recv.at[me], 1, device).start()

    def send_mixed(i):
        device, other = group(i)
        copy(m_send.at[other], m_recv.at[me], 2, device).start()

    def send_bias(i):
        device, s2 = row(i)
        copy(b_send, b_recv.at[s], 3, device).start()

    each(1, 16, send_taps)
    each(1, 64, send_grad)
    each(1, 64, send_mixed)
    each(1, 16, send_bias)
    h_recv[s] = h_send[me]
    g_recv[me] = g_send[me]
    m_recv[me] = m_send[me]
    b_recv[s] = b_send[...]

    h32[0:8, :] = jnp.zeros((8, 128), F32)
    g32[1024:1088, :] = jnp.zeros((64, 128), F32)
    mpad[0:128, :] = jnp.zeros((128, 128), BF16)
    rt[...] = jnp.zeros_like(rt)

    all_of(h_send, h_recv, 0, 15).wait()
    unpack_tiles(h_recv, h32, 8, 16)
    each(0, 4, lambda f: build_toeplitz(h32, f, t_ref.at[f]))

    all_of(g_send, g_recv, 1, 63).wait()
    unpack_tiles(g_recv, g32, 0, 64)

    def one_conv(f):
        build_gcat(g32, f, gcat, gt5.at[f])
        convolve(gcat, t_ref.at[f], acc)
        o32[pl.ds(f, 256, stride=4), :] = acc[...]

    each(0, 4, one_conv)

    def pack(i):
        rows = pl.ds(pl.multiple_of(128 * i, 8), 128)
        y_send[pl.ds(8 * i, 8)] = o32[rows, :].reshape(8, 16, 128).astype(BF16)

    each(0, 8, pack)

    def send_conv(i):
        device, other = group(i)
        copy(y_send.at[other], y_recv.at[me], 4, device).start()

    each(1, 64, send_conv)
    y_recv[me] = y_send[me]

    all_of(m_send, m_recv, 2, 63).wait()
    unpack_tiles(m_recv, m32, 0, 64)

    def one_cross(f):
        build_rt(m32, f, mpad, rt)
        correlate(rt, gt5.at[f], out)
        sum_diagonals(out, f, c_ref)

    each(0, 4, one_cross)

    def send_part(i):
        device, z2 = column(i)
        copy(c_ref.at[z2], c_recv.at[z], 5, device).start()

    each(1, 4, send_part)
    c_recv[z] = c_ref[z]
    all_of(c_ref, c_recv, 5, 3).wait()
    total = c_recv[0] + c_recv[1] + c_recv[2] + c_recv[3]
    c_sum[...] = (total * filter_scale).reshape(8, 8, 128)

    def send_cross(i):
        device, other = group(i)
        copy(c_sum.at[other // 8], c_last.at[me], 6, device).start()

    each(1, 64, send_cross)
    c_last[me] = c_sum[s // 2]

    all_of(y_send, y_recv, 4, 63).wait()
    conv = from_tiles(y_recv)
    for jj in range(4):
        rows = slice(128 * jj, 128 * jj + 128)
        mixed_grad = conv[jj] + gain_ref[...] * grad_ref[rows, :].astype(F32)
        key_out[rows, :] = (mixed_grad * value_ref[rows, :].astype(F32)).astype(BF16)
        value_out[rows, :] = (mixed_grad * key_ref[rows, :].astype(F32)).astype(BF16)

    copy(b_recv.at[pl.ds(0, 15)], b_recv.at[pl.ds(0, 15)], 3, group(1)[0]).wait()
    bias = jnp.sum(b_recv[...], axis=0) * bias_scale
    bias_out[...] = pltpu.roll(bias, (256 - 16 * s) % 256, 1)[0:1, 0:16]

    copy(c_last.at[pl.ds(0, 63)], c_last.at[pl.ds(0, 63)], 6, group(1)[0]).wait()
    parts = c_last[...]
    parts = jnp.where(s % 2 == 0, parts, turn(parts)).reshape(32, 2, 8, 128)
    rows = halves(parts[:, 0], turn(parts[:, 1])).reshape(256, 128)
    turned[...] = rows.T
    filter_out[...] = turned[pl.ds(pl.multiple_of(32 * x, 32), 32), :]


def per_device(scales, key_proj, value_proj, grad_out, filter_taps, skip_gain):
    vmem = pl.BlockSpec(memory_space=pltpu.VMEM)
    tiles = pltpu.VMEM((64, 16, 128), BF16)
    outs = pl.pallas_call(
        functools.partial(kernel, scales),
        out_shape=(
            jax.ShapeDtypeStruct((512, 256), BF16),
            jax.ShapeDtypeStruct((512, 256), BF16),
            jax.ShapeDtypeStruct((32, 256), F32),
            jax.ShapeDtypeStruct((1, 16), F32),
        ),
        in_specs=[vmem] * 5,
        out_specs=(vmem,) * 4,
        scratch_shapes=[
            tiles,
            tiles,
            tiles,
            pltpu.VMEM((8, 256), F32),
            tiles,
            tiles,
            pltpu.VMEM((16, 16, 128), BF16),
            pltpu.VMEM((16, 8, 256), F32),
            tiles,
            tiles,
            pltpu.VMEM((4, 64, 128), F32),
            pltpu.VMEM((4, 64, 128), F32),
            pltpu.VMEM((8, 8, 128), F32),
            pltpu.VMEM((64, 8, 128), F32),
            pltpu.VMEM((1088, 128), F32),
            pltpu.VMEM((1024, 128), F32),
            pltpu.VMEM((264, 128), F32),
            pltpu.VMEM((256, 512), BF16),
            pltpu.VMEM((4, 640, 256), BF16),
            pltpu.VMEM((4, 8, 256, 512), BF16),
            pltpu.VMEM((256, 128), F32),
            pltpu.VMEM((1024, 128), F32),
            pltpu.VMEM((384, 128), BF16),
            pltpu.VMEM((256, 2048), BF16),
            pltpu.VMEM((256, 512), F32),
            pltpu.VMEM((128, 256), F32),
            pltpu.SemaphoreType.DMA((7,)),
            pltpu.SemaphoreType.DMA((7,)),
        ],
        name="hyena_backward",
        compiler_params=pltpu.CompilerParams(
            collective_id=0, has_side_effects=True, vmem_limit_bytes=48 << 20
        ),
    )(key_proj, value_proj, grad_out, filter_taps, skip_gain.reshape(1, 256))
    return outs[0], outs[1], outs[2], outs[3].reshape(16)


def solution(mesh):
    in_specs = (P("seq", "chan"), P("seq", "chan"), P("seq", "chan"), P("seq", None), P("chan"))
    out_specs = (P("seq", "chan"), P("seq", "chan"), P(("seq", "chan"), None), P(("chan", "seq")))
    scales = (1.0 / math.sqrt(8192), 1.0 / math.sqrt(8192 * 16))
    return jax.shard_map(
        functools.partial(per_device, scales),
        mesh=mesh,
        in_specs=in_specs,
        out_specs=out_specs,
        check_vma=False,
    )
```

profile of v0, /device:TPU:1, one launch (start us, length us, event | category | flops | bytes accessed | tf_op | source)
XLA Modules:
  0.0 50.9 jit_solution(14065887761692738747)
XLA Ops:
  0.6 0.0 copy-start.4
  0.6 0.7 %copy-done.4 = f32[256]{0:T(256)S(1)} copy-done((f32[256]{0:T(256)S(1)}, f32[256]{0:T(256)}, u32[]{:S(2)}) %copy-start.4) | copy-done | bytes 1048
  1.3 0.0 copy-start
  1.3 0.9 %copy-done = bf16[512,256]{1,0:T(8,128)(2,1)S(1)} copy-done((bf16[512,256]{1,0:T(8,128)(2,1)S(1)}, bf16[512,256]{1,0:T(8,128)(2,1)}, u32[]{:S(2)}) %copy-start) | copy-done | bytes 262168
  2.3 0.0 copy-start.1
  2.3 0.9 %copy-done.1 = bf16[512,256]{1,0:T(8,128)(2,1)S(1)} copy-done((bf16[512,256]{1,0:T(8,128)(2,1)S(1)}, bf16[512,256]{1,0:T(8,128)(2,1)}, u32[]{:S(2)}) %copy-start.1) | copy-done | bytes 262168
  3.2 0.0 copy-start.2
  3.2 0.9 %copy-done.2 = bf16[512,256]{1,0:T(8,128)(2,1)S(1)} copy-done((bf16[512,256]{1,0:T(8,128)(2,1)S(1)}, bf16[512,256]{1,0:T(8,128)(2,1)}, u32[]{:S(2)}) %copy-start.2) | copy-done | bytes 262168
  4.2 0.0 copy-start.3
  4.2 0.9 %copy-done.3 = bf16[512,256]{1,0:T(8,128)(2,1)S(1)} copy-done((bf16[512,256]{1,0:T(8,128)(2,1)S(1)}, bf16[512,256]{1,0:T(8,128)(2,1)}, u32[]{:S(2)}) %copy-start.3) | copy-done | bytes 262168
  5.1 43.3 %hyena_backward.1 = (bf16[512,256]{1,0:T(8,128)(2,1)S(1)}, bf16[512,256]{1,0:T(8,128)(2,1)S(1)}, f32[32,256]{1,0:T(8,128)S(1)}, f32[1,16]{1,0:T(1,128)S(1)}) custom-call(bf16[512,256]{1,0:T(8,128)(2,1)S(1)} %copy-done, bf16[512,256]{1,0:T(8,128)(2,1)S(1)} %copy-done.1, bf16[512,256]{1,0:T(8,128)(2,1)S(1)} %copy-done.2, bf16[512,256]{1,0:T(8,128)(2,1)S(1)} %copy-done.3, ...), custom_call_target="tpu_custom_call" | custom-call | tf_op jit(solution)/shard_map/hyena_backward/pallas_call | solution.py:336
  48.4 0.7 %copy.13 = bf16[512,256]{1,0:T(8,128)(2,1)} copy(bf16[512,256]{1,0:T(8,128)(2,1)S(1)} %get-tuple-element.16) | data formatting | bytes 524288
  49.1 0.7 %copy.14 = bf16[512,256]{1,0:T(8,128)(2,1)} copy(bf16[512,256]{1,0:T(8,128)(2,1)S(1)} %get-tuple-element.17) | data formatting | bytes 524288
  49.8 0.6 %copy.15 = f32[32,256]{1,0:T(8,128)} copy(f32[32,256]{1,0:T(8,128)S(1)} %get-tuple-element.18) | data formatting | bytes 65536
  50.4 0.5 %copy.16 = f32[16]{0:T(128)} copy(f32[16]{0:T(128)S(1)} %bitcast.3) | data formatting | bytes 128
Async XLA Ops:
  0.6 0.7 %copy-start.4 = (f32[256]{0:T(256)S(1)}, f32[256]{0:T(256)}, u32[]{:S(2)}) copy-start(f32[256]{0:T(256)} %param.9) | copy-start | bytes 3076
  1.3 0.9 %copy-start = (bf16[512,256]{1,0:T(8,128)(2,1)S(1)}, bf16[512,256]{1,0:T(8,128)(2,1)}, u32[]{:S(2)}) copy-start(bf16[512,256]{1,0:T(8,128)(2,1)} %key_ref.1) | copy-start | bytes 786436
  2.3 0.9 %copy-start.1 = (bf16[512,256]{1,0:T(8,128)(2,1)S(1)}, bf16[512,256]{1,0:T(8,128)(2,1)}, u32[]{:S(2)}) copy-start(bf16[512,256]{1,0:T(8,128)(2,1)} %value_ref.1) | copy-start | bytes 786436
  3.2 0.9 %copy-start.2 = (bf16[512,256]{1,0:T(8,128)(2,1)S(1)}, bf16[512,256]{1,0:T(8,128)(2,1)}, u32[]{:S(2)}) copy-start(bf16[512,256]{1,0:T(8,128)(2,1)} %grad_ref.1) | copy-start | bytes 786436
  4.2 0.9 %copy-start.3 = (bf16[512,256]{1,0:T(8,128)(2,1)S(1)}, bf16[512,256]{1,0:T(8,128)(2,1)}, u32[]{:S(2)}) copy-start(bf16[512,256]{1,0:T(8,128)(2,1)} %taps_ref.1) | copy-start | bytes 786436
where the time goes:
time: 51.2 us; the launch traced here: 50.9 us
  Pallas kernels  43.3 us (85%)
  local copies, waits for them, and re-layouts  7 us (14%)
  between operations  0.65 us (1%)
    pallas_call x1, Pallas kernels, per_device(): pl.pallas_call(functools.partial(kernel, scales), out_shape=(jax.ShapeDty...  43.3 us
    unnamed x14, local copies, waits for them, and re-layouts  7 us

commit v1 on v0

v1 whole, which is shorter than its diff:
```python
import functools
import math

import jax
import jax.numpy as jnp
from jax import lax
from jax.experimental import pallas as pl
from jax.experimental.pallas import tpu as pltpu
from jax.sharding import PartitionSpec as P

MESH = pl.DeviceIdType.MESH
F32, BF16 = jnp.float32, jnp.bfloat16
NT = (((1,), (1,)), ((), ()))


def dot_nt(a, b):
    return lax.dot_general(a, b, NT, preferred_element_type=F32)


def iotas(rows, cols=128):
    lane = lax.broadcasted_iota(jnp.int32, (rows, cols), 1)
    return lane, lax.broadcasted_iota(jnp.int32, (rows, cols), 0)


def eye(size):
    lane, row = iotas(size, size)
    return jnp.where(lane == row, 1.0, 0.0).astype(BF16)


def halves(low, high):
    sub = lax.broadcasted_iota(jnp.int32, low.shape, 1)
    return jnp.where(sub < 4, low, high)


def turn(rows):
    return pltpu.roll(rows, 4, 1)


def to_tiles(block, tiles):
    flipped = dot_nt(eye(256), block).reshape(32, 8, 512)
    v = [flipped[:, :, 128 * jj : 128 * jj + 128] for jj in range(4)]
    even = jnp.concatenate([halves(v[0], turn(v[1])), halves(v[2], turn(v[3]))], axis=1)
    odd = jnp.concatenate([halves(turn(v[0]), v[1]), halves(turn(v[2]), v[3])], axis=1)
    tiles[...] = jnp.stack([even, odd], axis=1).reshape(64, 16, 128).astype(BF16)


def pair_rows(block):
    flipped = dot_nt(eye(256), block).reshape(32, 8, 512)
    sub = lax.broadcasted_iota(jnp.int32, (32, 8, 128), 1) // 2
    turned = [[pltpu.roll(flipped[:, :, 128 * jj : 128 * jj + 128], 2 * r, 1) if r else flipped[:, :, 128 * jj : 128 * jj + 128] for r in range(4)] for jj in range(4)]

    def merge(shift):
        rows = turned[0][-shift % 4]
        for jj in range(1, 4):
            rows = jnp.where(sub == jj, turned[jj][(jj - shift) % 4], rows)
        return rows

    return [[merge(2 * par + hf) for par in range(2)] for hf in range(2)]


def to_pair_tiles(grad, mixed, tiles):
    g, m = pair_rows(grad), pair_rows(mixed)
    for hf in range(2):
        both = [jnp.concatenate([g[hf][par], m[hf][par]], axis=1) for par in range(2)]
        tiles[hf] = jnp.stack(both, axis=1).reshape(64, 16, 128).astype(BF16)


def from_tiles(tiles):
    pairs = tiles[...].astype(F32).reshape(32, 32, 128)
    e0, e1, o0, o1 = (pairs[:, 8 * i : 8 * i + 8, :] for i in range(4))
    v = [halves(e0, turn(o0)), halves(turn(e0), o0), halves(e1, turn(o1)), halves(turn(e1), o1)]
    return [dot_nt(eye(128), one.reshape(256, 128).astype(BF16)) for one in v]


def unpack_taps(src, dst):
    for i in range(2):
        dst[8 + 128 * i : 136 + 128 * i, :] = src[8 * i : 8 * i + 8].astype(F32).reshape(128, 128)


def unpack_pairs(src, g32, m32):
    def one(i, c):
        rows = pl.ds(pl.multiple_of(128 * i, 128), 128)
        both = src[pl.ds(16 * i, 16)].astype(F32)
        g32[rows, :] = both[:, 0:8, :].reshape(128, 128)
        m32[rows, :] = both[:, 8:16, :].reshape(128, 128)
        return c

    lax.fori_loop(0, 4, one, 0)


def build_toeplitz(h32, f, t_ref, i):
    lane, row = iotas(128)
    mask = lane + row < 128
    e, par = i // 2, i % 2
    rows = [h32[pl.ds(8 + 4 * (4 * i + j - 1) + f, 1), :] for j in range(5)]
    for d0 in range(4):
        before = jnp.broadcast_to(rows[d0], (128, 128))
        here = jnp.broadcast_to(rows[d0 + 1], (128, 128))
        t = pltpu.roll(jnp.where(mask, here, before), 0, 1, stride=1, stride_axis=0)
        t_ref[e, 128 * par : 128 * par + 128, 128 * d0 : 128 * d0 + 128] = t.astype(BF16)


def build_gcat(g32, f, gcat, gt5):
    jj = lax.broadcasted_iota(jnp.int32, (256, 128), 0) % 4
    unit = eye(128)
    for d0 in range(5):
        block = g32[pl.ds(f + 2 * (d0 if d0 < 4 else 16), 256, stride=2), :]
        if 0 < d0 < 4:
            later = g32[pl.ds(f + 2 * (d0 + 12), 256, stride=2), :]
            block = jnp.where(jj + d0 < 4, block, later)
        block = block.astype(BF16)
        if d0 < 4:
            gcat[:, 128 * d0 : 128 * d0 + 128] = block
        gt5[128 * d0 : 128 * d0 + 128, :] = dot_nt(unit, block).astype(BF16)


def convolve(gcat, t_ref, acc):
    acc[...] = jnp.zeros_like(acc)
    for e in range(8):
        n = 256 - 32 * e
        y = dot_nt(gcat[32 * e : 256, :], t_ref[e])
        acc[0:n, :] += y[:, 0:128]
        acc[0 : n - 16, :] += y[16:, 128:256]


def build_rt(m32, f, mpad, rt):
    mpad[128:384, :] = m32[pl.ds(f, 256, stride=2), :].astype(BF16)
    lane, row = iotas(128)
    flip = jnp.where(lane == (row // 16) * 16 + 15 - row % 16, 1.0, 0.0).astype(BF16)
    for d in range(8):
        t = dot_nt(flip, mpad[128 - 16 * d : 384 - 16 * d, :]).astype(BF16)
        for a in range(8):
            piece = t[16 * a : 16 * a + 16, :]
            rt[16 * d : 16 * d + 16, 256 * a : 256 * a + 256] = piece
            rt[128 + 16 * d : 144 + 16 * d, 256 * a + 128 : 256 * a + 256] = piece[:, 0:128]


def correlate(rt, gt5, out, beside):
    for half in range(2):
        acc = None
        for a in range(8):
            rows = gt5[16 * a + 256 * half : 16 * a + 256 * half + 256, :]
            y = dot_nt(rt[:, 256 * a : 256 * a + 256], rows)
            acc = y if acc is None else acc + y
            beside(8 * half + a)
        out[:, 256 * half : 256 * half + 256] = acc


def sum_diagonals(out, f, c_ref):
    lane, row = iotas(16)
    mask = lane + row >= 15
    after = jnp.zeros((16, 128), F32)
    for d1 in reversed(range(16)):
        for d0 in reversed(range(4)):
            here = out[16 * d1 : 16 * d1 + 16, 128 * d0 : 128 * d0 + 128]
            z = pltpu.roll(jnp.where(mask, here, after), 113, 1, stride=1, stride_axis=0)
            after = here
            c_ref[d0, pl.ds(4 * d1 + f, 1), :] = jnp.sum(z[0:8] + z[8:16], axis=0, keepdims=True)


def sum_bias(g32, m32, b_send):
    parts = []
    for hf in range(2):

        def one(i, sums):
            rows = pl.ds(pl.multiple_of(32 * i, 32), 32)
            return sums + g32[hf, rows, :] * m32[hf, rows, :]

        sums = lax.fori_loop(0, 16, one, jnp.zeros((32, 128), F32)).reshape(4, 8, 128)
        sums = sums + turn(sums)
        parts.append(sums + pltpu.roll(sums, 2, 1))
    sub = lax.broadcasted_iota(jnp.int32, (4, 8, 128), 1)
    b_send[...] = jnp.where(sub // 2 % 2 == 0, parts[0], parts[1])


def kernel(
    filter_scale,
    key_ref,
    value_ref,
    grad_ref,
    taps_ref,
    y_recv,
    c_last,
    b_recv,
    key_in,
    value_in,
    grad_in,
    taps_in,
    h_send,
    h_recv,
    x_send,
    x_recv,
    b_send,
    y_send,
    c_ref,
    c_recv,
    c_sum,
    g32,
    m32,
    h32,
    gcat,
    gt5,
    t_ref,
    acc,
    o32,
    mpad,
    rt,
    out,
    loads,
    sends,
    recvs,
):
    s, k = lax.axis_index("seq"), lax.axis_index("chan")
    y, c = s // 4, s % 4
    z, x = k // 4, k % 4
    me = 4 * s + x

    def group(i):
        s2 = (y + i // 16) % 4 * 4 + (c + i // 4 % 4) % 4
        x2 = (x + i % 4) % 4
        return (s2, 4 * z + x2), 4 * s2 + x2

    def row(i):
        s2 = (y + i // 4) % 4 * 4 + (c + i % 4) % 4
        return (s2, k), s2

    def column(i):
        z2 = (z + i) % 4
        return (s, 4 * z2 + x), z2

    def copy(src, dst, sem, device):
        return pltpu.make_async_remote_copy(
            src_ref=src,
            dst_ref=dst,
            send_sem=sends.at[sem],
            recv_sem=recvs.at[sem],
            device_id=device,
            device_id_type=MESH,
        )

    def all_of(src, dst, sem, count):
        return copy(src.at[pl.ds(0, count)], dst.at[pl.ds(0, count)], sem, group(1)[0])

    def each(lo, hi, body):
        lax.fori_loop(lo, hi, lambda i, none: (body(i), none)[1], 0)

    def others(count, body):
        for i in reversed(range(1, count)):
            body(i)

    inputs = ((taps_ref, taps_in), (grad_ref, grad_in), (key_ref, key_in), (value_ref, value_in))
    fetches = [pltpu.make_async_copy(src, dst, loads.at[i]) for i, (src, dst) in enumerate(inputs)]
    for fetch in fetches:
        fetch.start()

    barrier = pltpu.get_barrier_semaphore()

    def greet(device):
        pl.semaphore_signal(barrier, inc=1, device_id=device, device_id_type=MESH)

    others(64, lambda i: greet(group(i)[0]))
    others(4, lambda i: greet(column(i)[0]))

    fetches[0].wait()
    to_tiles(taps_in[...], h_send)
    for fetch in fetches[1:]:
        fetch.wait()
    mixed = (key_in[...].astype(F32) * value_in[...].astype(F32)).astype(BF16)
    to_pair_tiles(grad_in[...], mixed, x_send)

    h32[0:8, :] = jnp.zeros((8, 128), F32)
    for hf in range(2):
        g32[hf, 512:544, :] = jnp.zeros((32, 128), F32)
    mpad[0:128, :] = jnp.zeros((128, 128), BF16)
    rt[...] = jnp.zeros_like(rt)

    pl.semaphore_wait(barrier, 66)

    def send_taps(i):
        device, s2 = row(i)
        copy(h_send.at[4 * s2 + x], h_recv.at[s], 0, device).start()

    def send_pairs(hf):
        def send(i):
            device, other = group(i)
            copy(x_send.at[hf, other], x_recv.at[hf, me], 1 + hf, device).start()

        return send

    others(16, send_taps)
    others(64, send_pairs(0))
    others(64, send_pairs(1))
    h_recv[s] = h_send[me]
    for hf in range(2):
        x_recv[hf, me] = x_send[hf, me]

    all_of(h_send, h_recv, 0, 15).wait()
    unpack_taps(h_recv, h32)

    for hf in range(2):
        all_of(x_send.at[hf], x_recv.at[hf], 1 + hf, 63).wait()
        unpack_pairs(x_recv.at[hf], g32.at[hf], m32.at[hf])

        def one_cross(f2):
            f = 2 * hf + f2
            build_gcat(g32.at[hf], f2, gcat.at[f], gt5)
            build_rt(m32.at[hf], f2, mpad, rt)
            correlate(rt, gt5, out, lambda i: build_toeplitz(h32, f, t_ref.at[f], i))
            sum_diagonals(out, f, c_ref)

        each(0, 2, one_cross)

    def send_part(i):
        device, z2 = column(i)
        copy(c_ref.at[z2], c_recv.at[z], 3, device).start()

    others(4, send_part)
    c_recv[z] = c_ref[z]

    sum_bias(g32, m32, b_send)

    def send_bias(i):
        x2 = (x + i) % 4
        copy(b_send.at[x2], b_recv.at[x], 4, (s, 4 * z + x2)).start()

    others(4, send_bias)

    def one_conv(f):
        convolve(gcat.at[f], t_ref.at[f], acc)
        o32[pl.ds(f, 256, stride=4), :] = acc[...]

    each(0, 4, one_conv)

    def pack(i):
        rows = pl.ds(pl.multiple_of(128 * i, 8), 128)
        y_send[pl.ds(8 * i, 8)] = o32[rows, :].reshape(8, 16, 128).astype(BF16)

    each(0, 8, pack)

    def send_conv(i):
        device, other = group(i)
        copy(y_send.at[other], y_recv.at[me], 5, device).start()

    others(64, send_conv)

    all_of(c_ref, c_recv, 3, 3).wait()
    total = c_recv[0] + c_recv[1] + c_recv[2] + c_recv[3]
    c_sum[...] = (total * filter_scale).reshape(16, 4, 128)

    def send_cross(i):
        device, other = group(i)
        copy(c_sum.at[other // 4], c_last.at[me], 6, device).start()

    others(64, send_cross)
    mine = [
        pltpu.make_async_copy(b_send.at[x], b_recv.at[x], loads.at[0]),
        pltpu.make_async_copy(y_send.at[me], y_recv.at[me], loads.at[1]),
        pltpu.make_async_copy(c_sum.at[s], c_last.at[me], loads.at[2]),
    ]
    for one in mine:
        one.start()
    for one in mine:
        one.wait()

    all_of(b_send, b_recv, 4, 3).wait()
    all_of(y_send, y_recv, 5, 63).wait()
    copy(c_last.at[pl.ds(0, 63)], c_last.at[pl.ds(0, 63)], 6, group(1)[0]).wait()


def finish(
    bias_scale,
    key_ref,
    value_ref,
    grad_ref,
    y_ref,
    c_ref,
    b_ref,
    gain_ref,
    key_out,
    value_out,
    filter_out,
    bias_out,
    key_in,
    value_in,
    grad_in,
    y_in,
    c_in,
    b_in,
    key_grad,
    value_grad,
    turned,
    bias_grad,
    loads,
    stores,
):
    x = lax.axis_index("chan") % 4
    inputs = (
        (y_ref, y_in),
        (grad_ref, grad_in),
        (value_ref, value_in),
        (key_ref, key_in),
        (c_ref, c_in),
        (b_ref, b_in),
    )
    fetches = [pltpu.make_async_copy(src, dst, loads.at[i]) for i, (src, dst) in enumerate(inputs)]
    for fetch in fetches:
        fetch.start()
    started = []

    def store(src, dst):
        started.append(pltpu.make_async_copy(src, dst, stores.at[len(started)]))
        started[-1].start()

    for fetch in fetches[:4]:
        fetch.wait()
    conv = from_tiles(y_in)
    for jj in range(4):
        rows = slice(128 * jj, 128 * jj + 128)
        mixed_grad = conv[jj] + gain_ref[...] * grad_in[rows, :].astype(F32)
        key_grad[rows, :] = (mixed_grad * value_in[rows, :].astype(F32)).astype(BF16)
        value_grad[rows, :] = (mixed_grad * key_in[rows, :].astype(F32)).astype(BF16)
    store(key_grad, key_out)
    store(value_grad, value_out)
    fetches[4].wait()
    turned[...] = c_in[...].reshape(256, 128).T
    store(turned.at[pl.ds(pl.multiple_of(32 * x, 32), 32), :], filter_out)
    fetches[5].wait()
    sums = b_in[...]
    sub = lax.broadcasted_iota(jnp.int32, (8, 128), 0)
    sums = jnp.concatenate([jnp.where(sub < 4, sums[0], sums[1]), jnp.where(sub < 4, sums[2], sums[3])], axis=0)
    bias_grad[...] = jnp.sum(sums.T, axis=0, keepdims=True) * bias_scale
    store(bias_grad, bias_out)
    for one in started:
        one.wait()


def per_device(scales, key_proj, value_proj, grad_out, filter_taps, skip_gain):
    bias_scale, filter_scale = scales
    vmem = pl.BlockSpec(memory_space=pltpu.VMEM)
    hbm = pl.BlockSpec(memory_space=pltpu.HBM)
    block = jax.ShapeDtypeStruct((512, 256), BF16)
    outs = pl.pallas_call(
        functools.partial(kernel, filter_scale),
        out_shape=(
            jax.ShapeDtypeStruct((64, 16, 128), BF16),
            jax.ShapeDtypeStruct((64, 4, 128), F32),
            jax.ShapeDtypeStruct((4, 8, 128), F32),
        ),
        in_specs=[hbm] * 4,
        out_specs=(hbm,) * 3,
        scratch_shapes=[
            pltpu.VMEM((512, 256), BF16),
            pltpu.VMEM((512, 256), BF16),
            pltpu.VMEM((512, 256), BF16),
            pltpu.VMEM((512, 256), BF16),
            pltpu.VMEM((64, 16, 128), BF16),
            pltpu.VMEM((16, 16, 128), BF16),
            pltpu.VMEM((2, 64, 16, 128), BF16),
            pltpu.VMEM((2, 64, 16, 128), BF16),
            pltpu.VMEM((4, 8, 128), F32),
            pltpu.VMEM((64, 16, 128), BF16),
            pltpu.VMEM((4, 64, 128), F32),
            pltpu.VMEM((4, 64, 128), F32),
            pltpu.VMEM((16, 4, 128), F32),
            pltpu.VMEM((2, 544, 128), F32),
            pltpu.VMEM((2, 512, 128), F32),
            pltpu.VMEM((264, 128), F32),
            pltpu.VMEM((4, 256, 512), BF16),
            pltpu.VMEM((640, 256), BF16),
            pltpu.VMEM((4, 8, 256, 512), BF16),
            pltpu.VMEM((256, 128), F32),
            pltpu.VMEM((1024, 128), F32),
            pltpu.VMEM((384, 128), BF16),
            pltpu.VMEM((256, 2048), BF16),
            pltpu.VMEM((256, 512), F32),
            pltpu.SemaphoreType.DMA((4,)),
            pltpu.SemaphoreType.DMA((7,)),
            pltpu.SemaphoreType.DMA((7,)),
        ],
        name="hyena_exchange",
        compiler_params=pltpu.CompilerParams(
            collective_id=0, has_side_effects=True, vmem_limit_bytes=60 << 20
        ),
    )(key_proj, value_proj, grad_out, filter_taps)
    key_grad, value_grad, filter_grad, bias_grad = pl.pallas_call(
        functools.partial(finish, bias_scale),
        out_shape=(
            block,
            block,
            jax.ShapeDtypeStruct((32, 256), F32),
            jax.ShapeDtypeStruct((1, 16), F32),
        ),
        in_specs=[hbm] * 6 + [vmem],
        out_specs=(hbm,) * 4,
        scratch_shapes=[
            pltpu.VMEM((512, 256), BF16),
            pltpu.VMEM((512, 256), BF16),
            pltpu.VMEM((512, 256), BF16),
            pltpu.VMEM((64, 16, 128), BF16),
            pltpu.VMEM((64, 4, 128), F32),
            pltpu.VMEM((4, 8, 128), F32),
            pltpu.VMEM((512, 256), BF16),
            pltpu.VMEM((512, 256), BF16),
            pltpu.VMEM((128, 256), F32),
            pltpu.VMEM((1, 16), F32),
            pltpu.SemaphoreType.DMA((6,)),
            pltpu.SemaphoreType.DMA((4,)),
        ],
        name="hyena_finish",
        compiler_params=pltpu.CompilerParams(vmem_limit_bytes=60 << 20),
    )(key_proj, value_proj, grad_out, *outs, skip_gain.reshape(1, 256))
    return key_grad, value_grad, filter_grad, bias_grad.reshape(16)


def solution(mesh):
    in_specs = (P("seq", "chan"), P("seq", "chan"), P("seq", "chan"), P("seq", None), P("chan"))
    out_specs = (P("seq", "chan"), P("seq", "chan"), P(("seq", "chan"), None), P(("chan", "seq")))
    scales = (1.0 / math.sqrt(8192), 1.0 / math.sqrt(8192 * 16))
    return jax.shard_map(
        functools.partial(per_device, scales),
        mesh=mesh,
        in_specs=in_specs,
        out_specs=out_specs,
        check_vma=False,
    )
```

time: 51.2 us -> 39.7 us (0.78)
  local copies, waits for them, and re-layouts: 7 us -> 0 us
  Pallas kernels: 43.3 us -> 38.9 us
    unnamed x14 -> x0, local copies, waits for them, and re-layouts: 7 us -> none
    pallas_call x1 -> x2, Pallas kernels: 43.3 us -> 38.9 us  [the longest x1 35.9 us: per_device(): pl.pallas_call(functools.partial(kernel, filter_scale), out_shape=(jax.Sh...]
where the time goes in v1:
time: 39.7 us; the launch traced here: 39.6 us
  Pallas kernels  38.9 us (98%)
  between operations  0.64 us (2%)
    pallas_call x1, Pallas kernels, per_device(): pl.pallas_call(functools.partial(kernel, filter_scale), out_shape=(jax.Sh...  35.9 us
    pallas_call x1, Pallas kernels, per_device(): pl.pallas_call(functools.partial(finish, bias_scale), out_shape=(block, b...  3.02 us

profile of v1, /device:TPU:1, one launch (start us, length us, event | category | flops | bytes accessed | tf_op | source)
XLA Modules:
  0.0 39.6 jit_solution(923911578072107499)
XLA Ops:
  0.6 35.9 %hyena_exchange.1 = (bf16[64,16,128]{2,1,0:T(8,128)(2,1)}, f32[64,4,128]{2,1,0:T(4,128)}, f32[4,8,128]{2,1,0:T(8,128)}) custom-call(bf16[512,256]{1,0:T(8,128)(2,1)} %key_ref.3, bf16[512,256]{1,0:T(8,128)(2,1)} %value_ref.3, bf16[512,256]{1,0:T(8,128)(2,1)} %grad_ref.3, bf16[512,256]{1,0:T(8,128)(2,1)} %taps_ref.1), custom_call_target="tpu_custom_call" | custom-call | tf_op jit(solution)/shard_map/hyena_exchange/pallas_call | solution.py:442
  36.5 3.0 %hyena_finish.1 = (bf16[512,256]{1,0:T(8,128)(2,1)}, bf16[512,256]{1,0:T(8,128)(2,1)}, f32[32,256]{1,0:T(8,128)}, f32[1,16]{1,0:T(1,128)}) custom-call(bf16[512,256]{1,0:T(8,128)(2,1)} %key_ref.3, bf16[512,256]{1,0:T(8,128)(2,1)} %value_ref.3, bf16[512,256]{1,0:T(8,128)(2,1)} %grad_ref.3, bf16[64,16,128]{2,1,0:T(8,128)(2,1)} %get-tuple-element.11.y_ref, ...), custom_call_target="tpu_custom_call" | custom-call | tf_op jit(solution)/shard_map/hyena_finish/pallas_call | solution.py:485

commit v2 on v1

--- a/solution.py
+++ b/solution.py
@@ -73,8 +73,9 @@
 
 
 def unpack_taps(src, dst):
-    for i in range(2):
-        dst[8 + 128 * i : 136 + 128 * i, :] = src[8 * i : 8 * i + 8].astype(F32).reshape(128, 128)
+    lane, row = iotas(128)
+    reverse = jnp.where(lane + row == 127, 1.0, 0.0).astype(BF16)
+    dst[8:264, :] = jnp.dot(src[...].reshape(256, 128), reverse, preferred_element_type=F32)
 
 
 def unpack_pairs(src, g32, m32):
@@ -90,14 +91,14 @@
 
 def build_toeplitz(h32, f, t_ref, i):
     lane, row = iotas(128)
-    mask = lane + row < 128
+    mask = lane + row >= 127
     e, par = i // 2, i % 2
     rows = [h32[pl.ds(8 + 4 * (4 * i + j - 1) + f, 1), :] for j in range(5)]
     for d0 in range(4):
         before = jnp.broadcast_to(rows[d0], (128, 128))
         here = jnp.broadcast_to(rows[d0 + 1], (128, 128))
-        t = pltpu.roll(jnp.where(mask, here, before), 0, 1, stride=1, stride_axis=0)
-        t_ref[e, 128 * par : 128 * par + 128, 128 * d0 : 128 * d0 + 128] = t.astype(BF16)
+        t = pltpu.roll(jnp.where(mask, here, before), 1, 1, stride=1, stride_axis=0)
+        t_ref[e, 128 * d0 : 128 * d0 + 128, 128 * par : 128 * par + 128] = t.astype(BF16)
 
 
 def build_gcat(g32, f, gcat, gt5):
@@ -118,7 +119,7 @@
     acc[...] = jnp.zeros_like(acc)
     for e in range(8):
         n = 256 - 32 * e
-        y = dot_nt(gcat[32 * e : 256, :], t_ref[e])
+        y = jnp.dot(gcat[32 * e : 256, :], t_ref[e], preferred_element_type=F32)
         acc[0:n, :] += y[:, 0:128]
         acc[0 : n - 16, :] += y[16:, 128:256]
 
@@ -146,7 +147,7 @@
         out[:, 256 * half : 256 * half + 256] = acc
 
 
-def sum_diagonals(out, f, c_ref):
+def sum_diagonals(out, f2, c_ref):
     lane, row = iotas(16)
     mask = lane + row >= 15
     after = jnp.zeros((16, 128), F32)
@@ -155,7 +156,7 @@
             here = out[16 * d1 : 16 * d1 + 16, 128 * d0 : 128 * d0 + 128]
             z = pltpu.roll(jnp.where(mask, here, after), 113, 1, stride=1, stride_axis=0)
             after = here
-            c_ref[d0, pl.ds(4 * d1 + f, 1), :] = jnp.sum(z[0:8] + z[8:16], axis=0, keepdims=True)
+            c_ref[d0, pl.ds(2 * d1 + f2, 1), :] = jnp.sum(z[0:8] + z[8:16], axis=0, keepdims=True)
 
 
 def sum_bias(g32, m32, b_send):
@@ -171,6 +172,17 @@
         parts.append(sums + pltpu.roll(sums, 2, 1))
     sub = lax.broadcasted_iota(jnp.int32, (4, 8, 128), 1)
     b_send[...] = jnp.where(sub // 2 % 2 == 0, parts[0], parts[1])
+
+
+def regroup(rows):
+    lane, row = iotas(64)
+    to = row % 4
+    result = rows
+    for step in range(1, 4):
+        moved = jnp.where(to + step < 4, pltpu.roll(rows, 64 - step, 0), pltpu.roll(rows, 4 - step, 0))
+        moved = pltpu.roll(moved, 32 * step, 1)
+        result = jnp.where((lane // 32 - to + 4) % 4 == step, moved, result)
+    return result
 
 
 def kernel(
@@ -179,13 +191,19 @@
     value_ref,
     grad_ref,
     taps_ref,
-    y_recv,
+    gain_ref,
+    key_out,
+    value_out,
     c_last,
     b_recv,
+    y_recv,
+    key_grad,
+    value_grad,
     key_in,
     value_in,
     grad_in,
     taps_in,
+    gain_in,
     h_send,
     h_recv,
     x_send,
@@ -193,8 +211,10 @@
     b_send,
     y_send,
     c_ref,
+    c_send,
     c_recv,
     c_sum,
+    c_mine,
     g32,
     m32,
     h32,
@@ -248,7 +268,13 @@
         for i in reversed(range(1, count)):
             body(i)
 
-    inputs = ((taps_ref, taps_in), (grad_ref, grad_in), (key_ref, key_in), (value_ref, value_in))
+    inputs = (
+        (taps_ref, taps_in),
+        (grad_ref, grad_in),
+        (key_ref, key_in),
+        (value_ref, value_in),
+        (gain_ref, gain_in),
+    )
     fetches = [pltpu.make_async_copy(src, dst, loads.at[i]) for i, (src, dst) in enumerate(inputs)]
     for fetch in fetches:
         fetch.start()
@@ -306,22 +332,23 @@
             build_gcat(g32.at[hf], f2, gcat.at[f], gt5)
             build_rt(m32.at[hf], f2, mpad, rt)
             correlate(rt, gt5, out, lambda i: build_toeplitz(h32, f, t_ref.at[f], i))
-            sum_diagonals(out, f, c_ref)
+            sum_diagonals(out, f2, c_ref)
 
         each(0, 2, one_cross)
-
-    def send_part(i):
-        device, z2 = column(i)
-        copy(c_ref.at[z2], c_recv.at[z], 3, device).start()
-
-    others(4, send_part)
-    c_recv[z] = c_ref[z]
+        c_send[hf] = c_ref[...].astype(BF16)
+
+        def send_part(i):
+            device, z2 = column(i)
+            copy(c_send.at[hf, z2], c_recv.at[hf, z], 3 + hf, device).start()
+
+        others(4, send_part)
+        c_recv[hf, z] = c_send[hf, z]
 
     sum_bias(g32, m32, b_send)
 
     def send_bias(i):
         x2 = (x + i) % 4
-        copy(b_send.at[x2], b_recv.at[x], 4, (s, 4 * z + x2)).start()
+        copy(b_send.at[x2], b_recv.at[x], 5, (s, 4 * z + x2)).start()
 
     others(4, send_bias)
 
@@ -339,149 +366,162 @@
 
     def send_conv(i):
         device, other = group(i)
-        copy(y_send.at[other], y_recv.at[me], 5, device).start()
+        copy(y_send.at[other], y_recv.at[me], 6, device).start()
 
     others(64, send_conv)
 
-    all_of(c_ref, c_recv, 3, 3).wait()
-    total = c_recv[0] + c_recv[1] + c_recv[2] + c_recv[3]
-    c_sum[...] = (total * filter_scale).reshape(16, 4, 128)
+    for hf in range(2):
+        all_of(c_send.at[hf], c_recv.at[hf], 3 + hf, 3).wait()
+        total = jnp.sum(c_recv[hf].astype(F32), axis=0) * filter_scale
+        c_sum[:, 2 * hf : 2 * hf + 2, :] = total.reshape(16, 2, 128)
+    c_mine[...] = regroup(c_sum[...].reshape(64, 128)).reshape(64, 1, 128)
 
     def send_cross(i):
         device, other = group(i)
-        copy(c_sum.at[other // 4], c_last.at[me], 6, device).start()
+        copy(c_mine.at[other], c_last.at[me], 7, device).start()
 
     others(64, send_cross)
+    y_recv[me] = y_send[me]
     mine = [
         pltpu.make_async_copy(b_send.at[x], b_recv.at[x], loads.at[0]),
-        pltpu.make_async_copy(y_send.at[me], y_recv.at[me], loads.at[1]),
-        pltpu.make_async_copy(c_sum.at[s], c_last.at[me], loads.at[2]),
+        pltpu.make_async_copy(c_mine.at[me], c_last.at[me], loads.at[1]),
+        pltpu.make_async_copy(key_grad, key_out, loads.at[2]),
+        pltpu.make_async_copy(value_grad, value_out, loads.at[3]),
     ]
-    for one in mine:
-        one.start()
+    mine[0].start()
+    mine[1].start()
+
+    all_of(y_send, y_recv, 6, 63).wait()
+    conv = from_tiles(y_recv)
+    for jj in range(4):
+        rows = slice(128 * jj, 128 * jj + 128)
+        mixed_grad = conv[jj] + gain_in[...] * grad_in[rows, :].astype(F32)
+        key_grad[rows, :] = (mixed_grad * value_in[rows, :].astype(F32)).astype(BF16)
+        value_grad[rows, :] = (mixed_grad * key_in[rows, :].astype(F32)).astype(BF16)
+    mine[2].start()
+    mine[3].start()
+
+    all_of(b_send, b_recv, 5, 3).wait()
+    copy(c_last.at[pl.ds(0, 63)], c_last.at[pl.ds(0, 63)], 7, group(1)[0]).wait()
     for one in mine:
         one.wait()
 
-    all_of(b_send, b_recv, 4, 3).wait()
-    all_of(y_send, y_recv, 5, 63).wait()
-    copy(c_last.at[pl.ds(0, 63)], c_last.at[pl.ds(0, 63)], 6, group(1)[0]).wait()
+
+def spread(parts):
+    lane, row = iotas(64, 256)
+    total = None
+    for f in range(4):
+        place = jnp.where(lane == 4 * row + f, 1.0, 0.0).astype(F32)
+        moved = jnp.dot(
+            parts[32 * f : 32 * f + 32, :], place, precision=lax.Precision.HIGHEST, preferred_element_type=F32
+        )
+        total = moved if total is None else total + moved
+    return total
 
 
 def finish(
     bias_scale,
     key_ref,
     value_ref,
-    grad_ref,
-    y_ref,
     c_ref,
     b_ref,
-    gain_ref,
     key_out,
     value_out,
     filter_out,
     bias_out,
+    c_in,
+    b_in,
     key_in,
     value_in,
-    grad_in,
-    y_in,
-    c_in,
-    b_in,
-    key_grad,
-    value_grad,
     turned,
     bias_grad,
     loads,
     stores,
 ):
-    x = lax.axis_index("chan") % 4
-    inputs = (
-        (y_ref, y_in),
-        (grad_ref, grad_in),
-        (value_ref, value_in),
-        (key_ref, key_in),
-        (c_ref, c_in),
-        (b_ref, b_in),
-    )
-    fetches = [pltpu.make_async_copy(src, dst, loads.at[i]) for i, (src, dst) in enumerate(inputs)]
-    for fetch in fetches:
-        fetch.start()
-    started = []
-
-    def store(src, dst):
-        started.append(pltpu.make_async_copy(src, dst, stores.at[len(started)]))
-        started[-1].start()
-
-    for fetch in fetches[:4]:
-        fetch.wait()
-    conv = from_tiles(y_in)
-    for jj in range(4):
-        rows = slice(128 * jj, 128 * jj + 128)
-        mixed_grad = conv[jj] + gain_ref[...] * grad_in[rows, :].astype(F32)
-        key_grad[rows, :] = (mixed_grad * value_in[rows, :].astype(F32)).astype(BF16)
-        value_grad[rows, :] = (mixed_grad * key_in[rows, :].astype(F32)).astype(BF16)
-    store(key_grad, key_out)
-    store(value_grad, value_out)
-    fetches[4].wait()
-    turned[...] = c_in[...].reshape(256, 128).T
-    store(turned.at[pl.ds(pl.multiple_of(32 * x, 32), 32), :], filter_out)
-    fetches[5].wait()
+    loaded = [
+        pltpu.make_async_copy(c_ref, c_in, loads.at[0]),
+        pltpu.make_async_copy(b_ref, b_in, loads.at[1]),
+        pltpu.make_async_copy(key_ref, key_in, loads.at[2]),
+        pltpu.make_async_copy(value_ref, value_in, loads.at[3]),
+    ]
+    stored = [
+        pltpu.make_async_copy(key_in, key_out, stores.at[0]),
+        pltpu.make_async_copy(value_in, value_out, stores.at[1]),
+        pltpu.make_async_copy(turned, filter_out, stores.at[2]),
+        pltpu.make_async_copy(bias_grad, bias_out, stores.at[3]),
+    ]
+    for one in loaded:
+        one.start()
+    loaded[0].wait()
+    turned[...] = spread(c_in[...].reshape(64, 128).T)
+    stored[2].start()
+    loaded[1].wait()
     sums = b_in[...]
     sub = lax.broadcasted_iota(jnp.int32, (8, 128), 0)
     sums = jnp.concatenate([jnp.where(sub < 4, sums[0], sums[1]), jnp.where(sub < 4, sums[2], sums[3])], axis=0)
     bias_grad[...] = jnp.sum(sums.T, axis=0, keepdims=True) * bias_scale
-    store(bias_grad, bias_out)
-    for one in started:
+    stored[3].start()
+    for load, store in zip(loaded[2:], stored):
+        load.wait()
+        store.start()
+    for one in stored:
         one.wait()
 
 
 def per_device(scales, key_proj, value_proj, grad_out, filter_taps, skip_gain):
     bias_scale, filter_scale = scales
-    vmem = pl.BlockSpec(memory_space=pltpu.VMEM)
     hbm = pl.BlockSpec(memory_space=pltpu.HBM)
     block = jax.ShapeDtypeStruct((512, 256), BF16)
     outs = pl.pallas_call(
         functools.partial(kernel, filter_scale),
         out_shape=(
-            jax.ShapeDtypeStruct((64, 16, 128), BF16),
-            jax.ShapeDtypeStruct((64, 4, 128), F32),
+            block,
+            block,
+            jax.ShapeDtypeStruct((64, 1, 128), F32),
             jax.ShapeDtypeStruct((4, 8, 128), F32),
         ),
-        in_specs=[hbm] * 4,
-        out_specs=(hbm,) * 3,
+        in_specs=[hbm] * 5,
+        out_specs=(hbm,) * 4,
         scratch_shapes=[
-            pltpu.VMEM((512, 256), BF16),
-            pltpu.VMEM((512, 256), BF16),
-            pltpu.VMEM((512, 256), BF16),
-            pltpu.VMEM((512, 256), BF16),
+            pltpu.VMEM((64, 16, 128), BF16),
+            pltpu.VMEM((512, 256), BF16),
+            pltpu.VMEM((512, 256), BF16),
+            pltpu.VMEM((512, 256), BF16),
+            pltpu.VMEM((512, 256), BF16),
+            pltpu.VMEM((512, 256), BF16),
+            pltpu.VMEM((512, 256), BF16),
+            pltpu.VMEM((1, 256), F32),
             pltpu.VMEM((64, 16, 128), BF16),
             pltpu.VMEM((16, 16, 128), BF16),
             pltpu.VMEM((2, 64, 16, 128), BF16),
             pltpu.VMEM((2, 64, 16, 128), BF16),
             pltpu.VMEM((4, 8, 128), F32),
             pltpu.VMEM((64, 16, 128), BF16),
-            pltpu.VMEM((4, 64, 128), F32),
-            pltpu.VMEM((4, 64, 128), F32),
+            pltpu.VMEM((4, 32, 128), F32),
+            pltpu.VMEM((2, 4, 32, 128), BF16),
+            pltpu.VMEM((2, 4, 32, 128), BF16),
             pltpu.VMEM((16, 4, 128), F32),
+            pltpu.VMEM((64, 1, 128), F32),
             pltpu.VMEM((2, 544, 128), F32),
             pltpu.VMEM((2, 512, 128), F32),
             pltpu.VMEM((264, 128), F32),
             pltpu.VMEM((4, 256, 512), BF16),
             pltpu.VMEM((640, 256), BF16),
-            pltpu.VMEM((4, 8, 256, 512), BF16),
+            pltpu.VMEM((4, 8, 512, 256), BF16),
             pltpu.VMEM((256, 128), F32),
             pltpu.VMEM((1024, 128), F32),
             pltpu.VMEM((384, 128), BF16),
             pltpu.VMEM((256, 2048), BF16),
             pltpu.VMEM((256, 512), F32),
-            pltpu.SemaphoreType.DMA((4,)),
-            pltpu.SemaphoreType.DMA((7,)),
-            pltpu.SemaphoreType.DMA((7,)),
+            pltpu.SemaphoreType.DMA((5,)),
+            pltpu.SemaphoreType.DMA((8,)),
+            pltpu.SemaphoreType.DMA((8,)),
         ],
         name="hyena_exchange",
         compiler_params=pltpu.CompilerParams(
             collective_id=0, has_side_effects=True, vmem_limit_bytes=60 << 20
         ),
-    )(key_proj, value_proj, grad_out, filter_taps)
+    )(key_proj, value_proj, grad_out, filter_taps, skip_gain.reshape(1, 256))
     key_grad, value_grad, filter_grad, bias_grad = pl.pallas_call(
         functools.partial(finish, bias_scale),
         out_shape=(
@@ -490,25 +530,21 @@
             jax.ShapeDtypeStruct((32, 256), F32),
             jax.ShapeDtypeStruct((1, 16), F32),
         ),
-        in_specs=[hbm] * 6 + [vmem],
+        in_specs=[hbm] * 4,
         out_specs=(hbm,) * 4,
         scratch_shapes=[
-            pltpu.VMEM((512, 256), BF16),
-            pltpu.VMEM((512, 256), BF16),
-            pltpu.VMEM((512, 256), BF16),
-            pltpu.VMEM((64, 16, 128), BF16),
-            pltpu.VMEM((64, 4, 128), F32),
+            pltpu.VMEM((64, 1, 128), F32),
             pltpu.VMEM((4, 8, 128), F32),
             pltpu.VMEM((512, 256), BF16),
             pltpu.VMEM((512, 256), BF16),
-            pltpu.VMEM((128, 256), F32),
+            pltpu.VMEM((32, 256), F32),
             pltpu.VMEM((1, 16), F32),
-            pltpu.SemaphoreType.DMA((6,)),
+            pltpu.SemaphoreType.DMA((4,)),
             pltpu.SemaphoreType.DMA((4,)),
         ],
         name="hyena_finish",
         compiler_params=pltpu.CompilerParams(vmem_limit_bytes=60 << 20),
-    )(key_proj, value_proj, grad_out, *outs, skip_gain.reshape(1, 256))
+    )(*outs)
     return key_grad, value_grad, filter_grad, bias_grad.reshape(16)
 
 

time: 39.7 us -> 37.2 us (0.937)
  Pallas kernels: 38.9 us -> 36.4 us
    pallas_call x1, Pallas kernels: 35.9 us -> 34.4 us  [per_device(): pl.pallas_call(functools.partial(kernel, filter_scale), out_shape=(block,...]
    pallas_call x1, Pallas kernels: 3.02 us -> 2.08 us  [per_device(): pl.pallas_call(functools.partial(finish, bias_scale), out_shape=(block, b...]
where the time goes in v2:
time: 37.2 us; the launch traced here: 37.1 us
  Pallas kernels  36.4 us (98%)
  between operations  0.64 us (2%)
    pallas_call x1, Pallas kernels, per_device(): pl.pallas_call(functools.partial(kernel, filter_scale), out_shape=(block,...  34.4 us
    pallas_call x1, Pallas kernels, per_device(): pl.pallas_call(functools.partial(finish, bias_scale), out_shape=(block, b...  2.08 us

profile of v2, /device:TPU:1, one launch (start us, length us, event | category | flops | bytes accessed | tf_op | source)
XLA Modules:
  0.0 37.1 jit_solution(9086693889070282414)
XLA Ops:
  0.6 34.4 %hyena_exchange.1 = (bf16[512,256]{1,0:T(8,128)(2,1)}, bf16[512,256]{1,0:T(8,128)(2,1)}, f32[64,1,128]{2,1,0:T(1,128)}, f32[4,8,128]{2,1,0:T(8,128)}) custom-call(bf16[512,256]{1,0:T(8,128)(2,1)} %key_ref.1, bf16[512,256]{1,0:T(8,128)(2,1)} %value_ref.1, bf16[512,256]{1,0:T(8,128)(2,1)} %grad_ref.1, bf16[512,256]{1,0:T(8,128)(2,1)} %taps_ref.1, f32[1,256]{1,0:T(1,128)} %bitcast.2), custom_call_target="tpu_custom_call" | custom-call | tf_op jit(solution)/shard_map/hyena_exchange/pallas_call | solution.py:475
  35.0 2.1 %hyena_finish.1 = (bf16[512,256]{1,0:T(8,128)(2,1)}, bf16[512,256]{1,0:T(8,128)(2,1)}, f32[32,256]{1,0:T(8,128)}, f32[1,16]{1,0:T(1,128)}) custom-call(bf16[512,256]{1,0:T(8,128)(2,1)} %get-tuple-element.12.key_ref, bf16[512,256]{1,0:T(8,128)(2,1)} %get-tuple-element.13.value_ref, f32[64,1,128]{2,1,0:T(1,128)} %get-tuple-element.14.c_ref, ...), custom_call_target="tpu_custom_call" | custom-call | tf_op jit(solution)/shard_map/hyena_finish/pallas_call | solution.py:525

commit v3 on v2

--- a/solution.py
+++ b/solution.py
@@ -11,6 +11,20 @@
 MESH = pl.DeviceIdType.MESH
 F32, BF16 = jnp.float32, jnp.bfloat16
 NT = (((1,), (1,)), ((), ()))
+
+
+def farthest_first(count):
+    def ring(step):
+        return min(step, 4 - step)
+
+    def hops(i):
+        if count == 4:
+            return ring(i)
+        x = i % 4 if count == 64 else 0
+        rest = i // 4 if count == 64 else i
+        return ring(rest // 4) + rest // 2 % 2 + ring(x)
+
+    return sorted(range(1, count), key=hops, reverse=True)
 
 
 def dot_nt(a, b):
@@ -265,7 +279,7 @@
         lax.fori_loop(lo, hi, lambda i, none: (body(i), none)[1], 0)
 
     def others(count, body):
-        for i in reversed(range(1, count)):
+        for i in farthest_first(count):
             body(i)
 
     inputs = (
@@ -297,7 +311,8 @@
     h32[0:8, :] = jnp.zeros((8, 128), F32)
     for hf in range(2):
         g32[hf, 512:544, :] = jnp.zeros((32, 128), F32)
-    mpad[0:128, :] = jnp.zeros((128, 128), BF16)
+    for f2 in range(2):
+        mpad[f2, 0:128, :] = jnp.zeros((128, 128), BF16)
     rt[...] = jnp.zeros_like(rt)
 
     pl.semaphore_wait(barrier, 66)
@@ -327,14 +342,13 @@
         all_of(x_send.at[hf], x_recv.at[hf], 1 + hf, 63).wait()
         unpack_pairs(x_recv.at[hf], g32.at[hf], m32.at[hf])
 
-        def one_cross(f2):
+        for f2 in range(2):
             f = 2 * hf + f2
-            build_gcat(g32.at[hf], f2, gcat.at[f], gt5)
-            build_rt(m32.at[hf], f2, mpad, rt)
-            correlate(rt, gt5, out, lambda i: build_toeplitz(h32, f, t_ref.at[f], i))
-            sum_diagonals(out, f2, c_ref)
-
-        each(0, 2, one_cross)
+            build_gcat(g32.at[hf], f2, gcat.at[f], gt5.at[f2])
+            build_rt(m32.at[hf], f2, mpad.at[f2], rt.at[f2])
+            correlate(rt.at[f2], gt5.at[f2], out.at[f2], functools.partial(build_toeplitz, h32, f, t_ref.at[f]))
+            sum_diagonals(out.at[f2], f2, c_ref)
+
         c_send[hf] = c_ref[...].astype(BF16)
 
         def send_part(i):
@@ -344,6 +358,24 @@
         others(4, send_part)
         c_recv[hf, z] = c_send[hf, z]
 
+    def one_conv(f):
+        convolve(gcat.at[f], t_ref.at[f], acc)
+        o32[pl.ds(f, 256, stride=4), :] = acc[...]
+
+    each(0, 4, one_conv)
+
+    def pack(i):
+        rows = pl.ds(pl.multiple_of(128 * i, 8), 128)
+        y_send[pl.ds(8 * i, 8)] = o32[rows, :].reshape(8, 16, 128).astype(BF16)
+
+    each(0, 8, pack)
+
+    def send_conv(i):
+        device, other = group(i)
+        copy(y_send.at[other], y_recv.at[me], 6, device).start()
+
+    others(64, send_conv)
+
     sum_bias(g32, m32, b_send)
 
     def send_bias(i):
@@ -352,23 +384,6 @@
 
     others(4, send_bias)
 
-    def one_conv(f):
-        convolve(gcat.at[f], t_ref.at[f], acc)
-        o32[pl.ds(f, 256, stride=4), :] = acc[...]
-
-    each(0, 4, one_conv)
-
-    def pack(i):
-        rows = pl.ds(pl.multiple_of(128 * i, 8), 128)
-        y_send[pl.ds(8 * i, 8)] = o32[rows, :].reshape(8, 16, 128).astype(BF16)
-
-    each(0, 8, pack)
-
-    def send_conv(i):
-        device, other = group(i)
-        copy(y_send.at[other], y_recv.at[me], 6, device).start()
-
-    others(64, send_conv)
 
     for hf in range(2):
         all_of(c_send.at[hf], c_recv.at[hf], 3 + hf, 3).wait()
@@ -506,13 +521,13 @@
             pltpu.VMEM((2, 512, 128), F32),
             pltpu.VMEM((264, 128), F32),
             pltpu.VMEM((4, 256, 512), BF16),
-            pltpu.VMEM((640, 256), BF16),
+            pltpu.VMEM((2, 640, 256), BF16),
             pltpu.VMEM((4, 8, 512, 256), BF16),
             pltpu.VMEM((256, 128), F32),
             pltpu.VMEM((1024, 128), F32),
-            pltpu.VMEM((384, 128), BF16),
-            pltpu.VMEM((256, 2048), BF16),
-            pltpu.VMEM((256, 512), F32),
+            pltpu.VMEM((2, 384, 128), BF16),
+            pltpu.VMEM((2, 256, 2048), BF16),
+            pltpu.VMEM((2, 256, 512), F32),
             pltpu.SemaphoreType.DMA((5,)),
             pltpu.SemaphoreType.DMA((8,)),
             pltpu.SemaphoreType.DMA((8,)),

time: 37.2 us -> 36.4 us (0.978)
  Pallas kernels: 36.4 us -> 35.7 us
    pallas_call x1, Pallas kernels: 34.4 us -> 33.6 us  [per_device(): pl.pallas_call(functools.partial(kernel, filter_scale), out_shape=(block,...]
where the time goes in v3:
time: 36.4 us; the launch traced here: 36.3 us
  Pallas kernels  35.7 us (98%)
  between operations  0.64 us (2%)
    pallas_call x1, Pallas kernels, per_device(): pl.pallas_call(functools.partial(kernel, filter_scale), out_shape=(block,...  33.6 us
    pallas_call x1, Pallas kernels, per_device(): pl.pallas_call(functools.partial(finish, bias_scale), out_shape=(block, b...  2.08 us

profile of v3, /device:TPU:1, one launch (start us, length us, event | category | flops | bytes accessed | tf_op | source)
XLA Modules:
  0.0 36.3 jit_solution(3836640795456701760)
XLA Ops:
  0.6 33.6 %hyena_exchange.1 = (bf16[512,256]{1,0:T(8,128)(2,1)}, bf16[512,256]{1,0:T(8,128)(2,1)}, f32[64,1,128]{2,1,0:T(1,128)}, f32[4,8,128]{2,1,0:T(8,128)}) custom-call(bf16[512,256]{1,0:T(8,128)(2,1)} %key_ref.1, bf16[512,256]{1,0:T(8,128)(2,1)} %value_ref.1, bf16[512,256]{1,0:T(8,128)(2,1)} %grad_ref.1, bf16[512,256]{1,0:T(8,128)(2,1)} %taps_ref.1, f32[1,256]{1,0:T(1,128)} %bitcast.2), custom_call_target="tpu_custom_call" | custom-call | tf_op jit(solution)/shard_map/hyena_exchange/pallas_call | solution.py:490
  34.2 2.1 %hyena_finish.1 = (bf16[512,256]{1,0:T(8,128)(2,1)}, bf16[512,256]{1,0:T(8,128)(2,1)}, f32[32,256]{1,0:T(8,128)}, f32[1,16]{1,0:T(1,128)}) custom-call(bf16[512,256]{1,0:T(8,128)(2,1)} %get-tuple-element.12.key_ref, bf16[512,256]{1,0:T(8,128)(2,1)} %get-tuple-element.13.value_ref, f32[64,1,128]{2,1,0:T(1,128)} %get-tuple-element.14.c_ref, ...), custom_call_target="tpu_custom_call" | custom-call | tf_op jit(solution)/shard_map/hyena_finish/pallas_call | solution.py:540

commit v4 on v3

--- a/solution.py
+++ b/solution.py
@@ -249,13 +249,18 @@
     z, x = k // 4, k % 4
     me = 4 * s + x
 
+    def place(i):
+        z_lo = 1 - c // 2 if i // 2 % 2 else c // 2
+        core = 1 - c % 2 if i % 2 else c % 2
+        return (y + i // 4) % 4 * 4 + z_lo * 2 + core
+
     def group(i):
-        s2 = (y + i // 16) % 4 * 4 + (c + i // 4 % 4) % 4
+        s2 = place(i // 4)
         x2 = (x + i % 4) % 4
         return (s2, 4 * z + x2), 4 * s2 + x2
 
     def row(i):
-        s2 = (y + i // 4) % 4 * 4 + (c + i % 4) % 4
+        s2 = place(i)
         return (s2, k), s2
 
     def column(i):
@@ -330,6 +335,7 @@
 
     others(16, send_taps)
     others(64, send_pairs(0))
+    all_of(x_send.at[0], x_recv.at[0], 1, 63).wait_send()
     others(64, send_pairs(1))
     h_recv[s] = h_send[me]
     for hf in range(2):
@@ -339,7 +345,10 @@
     unpack_taps(h_recv, h32)
 
     for hf in range(2):
-        all_of(x_send.at[hf], x_recv.at[hf], 1 + hf, 63).wait()
+        pair = all_of(x_send.at[hf], x_recv.at[hf], 1 + hf, 63)
+        pair.wait_recv()
+        if hf == 1:
+            pair.wait_send()
         unpack_pairs(x_recv.at[hf], g32.at[hf], m32.at[hf])
 
         for f2 in range(2):
@@ -358,11 +367,9 @@
         others(4, send_part)
         c_recv[hf, z] = c_send[hf, z]
 
-    def one_conv(f):
-        convolve(gcat.at[f], t_ref.at[f], acc)
-        o32[pl.ds(f, 256, stride=4), :] = acc[...]
-
-    each(0, 4, one_conv)
+    for f in range(4):
+        convolve(gcat.at[f], t_ref.at[f], acc.at[f])
+        o32[pl.ds(f, 256, stride=4), :] = acc[f]
 
     def pack(i):
         rows = pl.ds(pl.multiple_of(128 * i, 8), 128)
@@ -423,15 +430,18 @@
 
 
 def spread(parts):
+    high = parts.astype(BF16)
+    rest = parts - high.astype(F32)
+    middle = rest.astype(BF16)
+    low = (rest - middle.astype(F32)).astype(BF16)
     lane, row = iotas(64, 256)
-    total = None
+    total = jnp.zeros((96, 256), F32)
     for f in range(4):
-        place = jnp.where(lane == 4 * row + f, 1.0, 0.0).astype(F32)
-        moved = jnp.dot(
-            parts[32 * f : 32 * f + 32, :], place, precision=lax.Precision.HIGHEST, preferred_element_type=F32
-        )
-        total = moved if total is None else total + moved
-    return total
+        rows = slice(32 * f, 32 * f + 32)
+        terms = jnp.concatenate([high[rows], middle[rows], low[rows]], axis=0)
+        place = jnp.where(lane == 4 * row + f, 1.0, 0.0).astype(BF16)
+        total = total + jnp.dot(terms, place, preferred_element_type=F32)
+    return (total[64:96] + total[32:64]) + total[0:32]
 
 
 def finish(
@@ -523,7 +533,7 @@
             pltpu.VMEM((4, 256, 512), BF16),
             pltpu.VMEM((2, 640, 256), BF16),
             pltpu.VMEM((4, 8, 512, 256), BF16),
-            pltpu.VMEM((256, 128), F32),
+            pltpu.VMEM((4, 256, 128), F32),
             pltpu.VMEM((1024, 128), F32),
             pltpu.VMEM((2, 384, 128), BF16),
             pltpu.VMEM((2, 256, 2048), BF16),

time: 36.4 us -> 36.5 us (level)
  no operation moved by 1% of the time
where the time goes in v4:
time: 36.5 us; the launch traced here: 36.3 us
  Pallas kernels  35.7 us (98%)
  between operations  0.64 us (2%)
    pallas_call x1, Pallas kernels, per_device(): pl.pallas_call(functools.partial(kernel, filter_scale), out_shape=(block,...  33.7 us
    pallas_call x1, Pallas kernels, per_device(): pl.pallas_call(functools.partial(finish, bias_scale), out_shape=(block, b...  2.02 us

profile of v4, /device:TPU:1, one launch (start us, length us, event | category | flops | bytes accessed | tf_op | source)
XLA Modules:
  0.0 36.3 jit_solution(17162993618549046127)
XLA Ops:
  0.6 33.7 %hyena_exchange.1 = (bf16[512,256]{1,0:T(8,128)(2,1)}, bf16[512,256]{1,0:T(8,128)(2,1)}, f32[64,1,128]{2,1,0:T(1,128)}, f32[4,8,128]{2,1,0:T(8,128)}) custom-call(bf16[512,256]{1,0:T(8,128)(2,1)} %key_ref.1, bf16[512,256]{1,0:T(8,128)(2,1)} %value_ref.1, bf16[512,256]{1,0:T(8,128)(2,1)} %grad_ref.1, bf16[512,256]{1,0:T(8,128)(2,1)} %taps_ref.1, f32[1,256]{1,0:T(1,128)} %bitcast.2), custom_call_target="tpu_custom_call" | custom-call | tf_op jit(solution)/shard_map/hyena_exchange/pallas_call | solution.py:500
  34.3 2.0 %hyena_finish.1 = (bf16[512,256]{1,0:T(8,128)(2,1)}, bf16[512,256]{1,0:T(8,128)(2,1)}, f32[32,256]{1,0:T(8,128)}, f32[1,16]{1,0:T(1,128)}) custom-call(bf16[512,256]{1,0:T(8,128)(2,1)} %get-tuple-element.12.key_ref, bf16[512,256]{1,0:T(8,128)(2,1)} %get-tuple-element.13.value_ref, f32[64,1,128]{2,1,0:T(1,128)} %get-tuple-element.14.c_ref, ...), custom_call_target="tpu_custom_call" | custom-call | tf_op jit(solution)/shard_map/hyena_finish/pallas_call | solution.py:550
